TPU v7x, 32 devices: a whole 2x2x4 slice. The times are simulated.
32 devices in a mesh: tm: 2 (over x), height: 8 (over z, y), batch: 2 (over core).
Axes of the slice: x: 2, y: 2, z: 4, core: 2. Of those that a mesh axis runs over, the one named last changes fastest.
Arguments:
- conv_input: bfloat16 [2, 4, 8, 64, 384], P('batch', 'tm', 'height'), may hold values from -6 to 6
- saved: bfloat16 [2, 4, 8, 64, 384], P('batch', 'tm', 'height'), may hold values from -6 to 6
- cotangent: bfloat16 [2, 4, 8, 64, 384], P('batch', 'tm', 'height'), may hold values from -6 to 6
- gain: float32 [384], replicated, may hold values from 0.1 to 1.9
- w_conv: bfloat16 [3, 3, 3, 384, 384], replicated, may hold values from -0.0625 to 0.0625
- w_qkv: bfloat16 [384, 1152], replicated, may hold values from -4 to 4
- w_out: bfloat16 [384, 384], replicated, may hold values from -0.3125 to 0.3125
Outputs:
- input_grad: bfloat16 [2, 4, 8, 64, 384], P('batch', 'tm', 'height')
- weight_grad: float32 [384, 27, 384], P('height')
All inputs are finite; a program needn't handle non-finite values.
Results may differ from a plain program's by a relative error of at most 0.015.
Values may be sent and summed in bfloat16 or wider, within the bound.
A program may use at most 128 MiB of HBM per device.

v0:
```python
import math

import jax
import jax.numpy as jnp
from jax import lax
from jax.sharding import PartitionSpec as P

EPS = 1e-06


def with_halo(x, sides, width):
    for axis, dim in sides:
        size, length = (lax.axis_size(axis), x.shape[dim])
        up = [(i, (i + 1) % size) for i in range(size - 1)]
        down = [(j, i) for i, j in up]
        last = lax.slice_in_dim(x, length - width, length, axis=dim)
        leading = lax.slice_in_dim(x, 0, width, axis=dim)
        before = lax.ppermute(last, axis, up)
        after = lax.ppermute(leading, axis, down)
        x = jnp.concatenate([before, x, after], axis=dim)
    return x


def from_behind(value, axis, steps):
    count = lax.axis_size(axis)
    leading, last = (max(0, -steps), min(count, count - steps))
    return lax.ppermute(value, axis, [(source, source + steps) for source in range(leading, last)])


def local(conv_input, saved, cotangent, gain, w_conv, w_qkv, w_out):
    chans = saved.shape[-1]
    frames_dev = saved.shape[1]
    band_rows = saved.shape[2]
    columns = saved.shape[3]
    n_height = lax.axis_size("height")
    n_time = lax.axis_size("tm")
    n_clips = lax.axis_size("batch")
    local_pos = band_rows * columns
    scale = 1.0 / math.sqrt(chans)
    hidden = saved[0].astype(jnp.float32)
    inverse = lax.rsqrt(jnp.mean(hidden * hidden, -1, keepdims=True) + EPS)
    normed = (hidden * inverse * gain).astype(jnp.bfloat16)
    normed_rows = normed.reshape(frames_dev, local_pos, chans)
    queries = jnp.dot(normed_rows, w_qkv[:, :chans], preferred_element_type=jnp.float32).astype(
        jnp.bfloat16
    )
    all_normed = lax.all_gather(normed_rows, "height", axis=1, tiled=True)
    key_vals = jnp.dot(all_normed, w_qkv[:, chans:], preferred_element_type=jnp.float32).astype(
        jnp.bfloat16
    )
    keys = key_vals[..., :chans]
    values = key_vals[..., chans:]
    grad_out = jnp.dot(
        cotangent[0].reshape(frames_dev, local_pos, chans),
        w_out.T,
        preferred_element_type=jnp.float32,
    ).astype(jnp.bfloat16)
    scores = jnp.einsum("fqc,fkc->fqk", queries, keys, preferred_element_type=jnp.float32) * scale
    probs = jax.nn.softmax(scores, axis=-1)
    probs_low = probs.astype(jnp.bfloat16)
    grad_probs = jnp.einsum("fqc,fkc->fqk", grad_out, values, preferred_element_type=jnp.float32)
    delta = jnp.sum(probs * grad_probs, -1, keepdims=True)
    grad_scores = (probs * (grad_probs - delta) * scale).astype(jnp.bfloat16)
    grad_q = jnp.einsum(
        "fqk,fkc->fqc", grad_scores, keys, preferred_element_type=jnp.float32
    ).astype(jnp.bfloat16)
    grad_k = jnp.einsum("fqk,fqc->kfc", grad_scores, queries, preferred_element_type=jnp.float32)
    grad_v = jnp.einsum("fqk,fqc->kfc", probs_low, grad_out, preferred_element_type=jnp.float32)
    owned = lax.psum_scatter(
        jnp.concatenate([grad_k, grad_v], -1)
        .reshape(local_pos * lax.axis_size("height"), -1)
        .astype(jnp.bfloat16),
        "height",
        scatter_dimension=0,
        tiled=True,
    ).astype(jnp.float32)
    owned_kv = (
        owned.reshape(local_pos, frames_dev, 2 * chans).transpose(1, 0, 2).astype(jnp.bfloat16)
    )
    grad_qkv = jnp.concatenate([grad_q, owned_kv], -1)
    grad_normed = jnp.dot(grad_qkv, w_qkv.T, preferred_element_type=jnp.float32)
    scaled = grad_normed.reshape(hidden.shape) * gain
    grad_saved = (
        cotangent[0].astype(jnp.float32)
        + inverse
        * (scaled - hidden * inverse * inverse * jnp.mean(scaled * hidden, -1, keepdims=True))
    ).astype(jnp.bfloat16)
    rows_ext = with_halo(grad_saved, (("height", 1),), 1)
    following = from_behind(rows_ext, "tm", -1)
    extended = jnp.concatenate([rows_ext, following], 0)
    extended = jnp.pad(extended, ((0, 0), (0, 0), (1, 1), (0, 0)))
    windows = []
    for tap_t in range(3):
        for tap_r in range(3):
            for tap_c in range(3):
                windows.append(
                    extended[
                        2 - tap_t : 2 - tap_t + frames_dev,
                        2 - tap_r : 2 - tap_r + band_rows,
                        2 - tap_c : 2 - tap_c + columns,
                    ].reshape(-1, chans)
                )
    stacked = jnp.stack(windows, 0)
    kernel = w_conv.reshape(27, chans, chans)
    grad_input = jnp.einsum("trc,tdc->rd", stacked, kernel, preferred_element_type=jnp.float32)
    grad_input = grad_input.reshape(conv_input.shape).astype(jnp.bfloat16)
    norm_factor = 1.0 / math.sqrt(n_clips * n_time * frames_dev * n_height * band_rows * columns)
    left = conv_input[0].reshape(-1, chans)
    term = (
        jnp.einsum("rd,tre->dte", left, stacked, preferred_element_type=jnp.float32) * norm_factor
    )
    banded = lax.psum_scatter(term.astype(jnp.bfloat16), "height", scatter_dimension=0, tiled=True)
    weight_grad = lax.psum(banded, ("tm", "batch")).astype(jnp.float32)
    return (grad_input, weight_grad)


def solution(mesh):
    return jax.shard_map(
        local,
        mesh=mesh,
        in_specs=(
            P("batch", "tm", "height", None, None),
            P("batch", "tm", "height", None, None),
            P("batch", "tm", "height", None, None),
            P(),
            P(),
            P(),
            P(),
        ),
        out_specs=(P("batch", "tm", "height", None, None), P("height", None, None)),
        check_vma=False,
    )
```

profile of v0, /device:TPU:0, one launch (start us, length us, event | category | flops | bytes accessed | tf_op | source)
XLA Modules:
  0.0 397.8 jit_solution(4699989158646230819)
XLA Ops:
  7.2 1.0 fusion.41
  8.3 1.0 fusion.34
  9.3 33.8 %all_gather.3 = bf16[2,512,384]{2,1,0:T(8,128)(2,1)S(1)} all-gather(bf16[2,64,384]{2,1,0:T(8,128)(2,1)S(1)} %fusion.34), channel_id=1, replica_groups=mesh['tm'=2,'height'=8,'batch'=2] {'height'}, dimensions={1}, use_global_device_ids=true | all-gather | bytes 884736 | tf_op jit(solution)/shard_map/all_gather | solution.py:47
  43.0 1.2 convolution_convert_fusion.5
  44.2 2.0 convolution_convert_fusion
  47.6 1.4 fusion.4
  49.1 1.6 fusion.3
  50.7 1.5 pad_maximum_fusion
  52.2 1.6 copy.74
  53.8 1.8 convolution_convert_fusion.3
  55.6 64.2 %reduce-scatter.3.cloned.1.call-done = bf16[64,1536]{1,0:T(8,128)(2,1)} async-done(((bf16[512,1536]{1,0:T(8,128)(2,1)}), bf16[64,1536]{1,0:T(8,128)(2,1)}) %reduce-scatter.3.cloned.1.call-update) | async-done | bytes 196624 | tf_op jit(solution)/shard_map/reduce_scatter | solution.py:69
  119.8 0.9 copy.110
  121.4 1.3 collective-permute-start.1
  122.7 4.6 %collective-permute-start = (bf16[2,1,64,384]{3,2,0,1:T(8,128)(2,1)S(1)}, bf16[2,1,64,384]{3,2,0,1:T(8,128)(2,1)S(1)}, u32[]{:S(2)}, u32[]{:S(2)}) collective-permute-start(bf16[2,1,64,384]{3,2,0,1:T(8,128)(2,1)S(1)} %bitcast.126), channel_id=1, source_target_pairs={{0,2},{2,4},{4,6},{6,8},{8,10},{10,12},{12,14},{1,3},{3,5},{5,7},{... | collective-permute-start | bytes 294920 | tf_op jit(solution)/shard_map/ppermute | solution.py:18
  127.9 1.5 collective-permute-done
  129.5 1.3 collective-permute-start.2
  131.1 7.7 %collective-permute-done.2 = bf16[2,3,64,384]{3,2,0,1:T(8,128)(2,1)S(1)} collective-permute-done((bf16[2,3,64,384]{3,2,0,1:T(8,128)(2,1)S(1)}, bf16[2,3,64,384]{3,2,0,1:T(8,128)(2,1)S(1)}, u32[]{:S(2)}, u32[]{:S(2)}) %collective-permute-start.2) | collective-permute-done | bytes 294944 | tf_op jit(solution)/shard_map/ppermute | solution.py:27
  140.9 0.8 copy.77
  141.6 0.8 copy.76
  144.0 0.8 copy.81
  146.3 0.8 copy.85
  147.8 0.8 copy.88
  149.4 0.8 copy.90
  150.1 0.8 copy.91
  151.6 0.8 copy.94
  153.1 0.7 copy.97
  154.0 0.8 copy.89
  155.6 1.0 constant_dynamic-update-slice_fusion.26
  156.6 0.9 constant_dynamic-update-slice_fusion.25
  157.5 0.9 constant_dynamic-update-slice_fusion.24
  158.4 0.9 constant_dynamic-update-slice_fusion.23
  159.3 0.9 constant_dynamic-update-slice_fusion.22
  160.2 0.9 constant_dynamic-update-slice_fusion.21
  161.1 0.9 constant_dynamic-update-slice_fusion.20
  162.0 0.9 constant_dynamic-update-slice_fusion.19
  162.9 0.9 constant_dynamic-update-slice_fusion.18
  163.8 0.9 constant_dynamic-update-slice_fusion.17
  164.7 0.9 constant_dynamic-update-slice_fusion.16
  165.7 0.9 constant_dynamic-update-slice_fusion.15
  166.6 0.9 constant_dynamic-update-slice_fusion.14
  167.5 0.9 constant_dynamic-update-slice_fusion.13
  168.8 4.3 %fusion.2 = bf16[384,27,384]{0,2,1:T(8,128)(2,1)} fusion(bf16[27,128,384]{1,2,0:T(8,128)(2,1)S(1)} %constant_dynamic-update-slice_fusion, bf16[128,384,1]{1,0,2:T(8,128)(2,1)S(1)} %bitcast.158), kind=kOutput, calls=%fused_computation.3 | convolution fusion | flops 1027178496 | bytes 10715136 | tf_op jit(solution)/shard_map/rd,tre->dte/dot_general | solution.py:110
  173.1 12.9 %copy.104 = bf16[384,27,384]{2,1,0:T(8,128)(2,1)} copy(bf16[384,27,384]{0,2,1:T(8,128)(2,1)} %fusion.2) | data formatting | bytes 15925248 | tf_op jit(solution)/shard_map/convert_element_type | solution.py:112
  186.0 3.3 copy.103
  189.3 160.1 %reduce-scatter.5.cloned.1.call-done = bf16[48,27,384]{2,1,0:T(8,128)(2,1)} async-done(((bf16[384,27,384]{2,1,0:T(8,128)(2,1)}), bf16[48,27,384]{2,1,0:T(8,128)(2,1)}) %reduce-scatter.5.cloned.1.call-update) | async-done | bytes 995344 | tf_op jit(solution)/shard_map/reduce_scatter | solution.py:112
  349.4 7.1 %fusion.12 = bf16[1,2,1,64,384]{4,3,2,1,0:T(8,128)(2,1)} fusion(bf16[2,64,384,27]{2,1,0,3:T(8,128)(2,1)} %bitcast.122, bf16[27,384,384,1]{2,1,3,0:T(8,128)(2,1)} %bitcast.123), kind=kOutput, calls=%fused_computation.23 | convolution fusion | flops 1019265024 | bytes 10715136 | tf_op jit(solution)/shard_map/trc,tdc->rd/dot_general | solution.py:105
  356.5 31.8 %all-reduce.3.cloned.1.call-done = bf16[48,27,384]{2,1,0:T(8,128)(2,1)} async-done(((bf16[48,27,384]{2,1,0:T(8,128)(2,1)}), bf16[48,27,384]{2,1,0:T(8,128)(2,1)}) %all-reduce.3.cloned.1.call-update) | async-done | bytes 995344 | tf_op jit(solution)/shard_map/psum | solution.py:113
  388.3 2.9 copy.106
  (81 shorter events, 12.5 us)
Async XLA Ops:
  7.2 39.1 %copy-start = (bf16[384,384]{1,0:T(8,128)(2,1)S(1)}, bf16[384,384]{1,0:T(8,128)(2,1)}, u32[]{:S(2)}) copy-start(bf16[384,384]{1,0:T(8,128)(2,1)} %param.13) | copy-start | bytes 884740
  7.2 39.1 %copy-start.10 = (bf16[1,2,1,64,384]{4,3,2,1,0:T(8,128)(2,1)S(1)}, bf16[1,2,1,64,384]{4,3,2,1,0:T(8,128)(2,1)}, u32[]{:S(2)}) copy-start(bf16[1,2,1,64,384]{4,3,2,1,0:T(8,128)(2,1)} %param.9) | copy-start | bytes 294916
  7.2 112.6 %reduce-scatter.3.cloned.1.call-start = ((), (), s32[]{:S(2)}) async-start(), calls=%async_computation.2 | async-start | bytes 1769472 | tf_op jit(solution)/shard_map/reduce_scatter | solution.py:69
  46.9 2.2 copy-start.12
  47.6 1.4 copy-start.11
  53.7 67.0 %copy-start.1 = (bf16[384,1152]{1,0:T(8,128)(2,1)S(1)}, bf16[384,1152]{1,0:T(8,128)(2,1)}, u32[]{:S(2)}) copy-start(bf16[384,1152]{1,0:T(8,128)(2,1)} %param.12) | copy-start | bytes 2654212
  53.7 67.0 %copy-start.2 = (bf16[1,2,1,64,384]{4,3,2,1,0:T(8,128)(2,1)S(1)}, bf16[1,2,1,64,384]{4,3,2,1,0:T(8,128)(2,1)}, u32[]{:S(2)}) copy-start(bf16[1,2,1,64,384]{4,3,2,1,0:T(8,128)(2,1)} %param.8) | copy-start | bytes 294916
  53.7 67.0 %copy-start.14 = (f32[384]{0:T(512)S(1)}, f32[384]{0:T(512)}, u32[]{:S(2)}) copy-start(f32[384]{0:T(512)} %param.10) | copy-start | bytes 4612
  53.8 295.6 %reduce-scatter.5.cloned.1.call-start = ((), (), s32[]{:S(2)}) async-start(), calls=%async_computation.3 | async-start | bytes 10616832 | tf_op jit(solution)/shard_map/reduce_scatter | solution.py:112
  121.4 6.5 %collective-permute-start.1 = (bf16[2,1,64,384]{3,2,0,1:T(8,128)(2,1)S(1)}, bf16[2,1,64,384]{3,2,0,1:T(8,128)(2,1)S(1)}, u32[]{:S(2)}, u32[]{:S(2)}) collective-permute-start(bf16[2,1,64,384]{3,2,0,1:T(8,128)(2,1)S(1)} %bitcast.125), channel_id=1, source_target_pairs={{2,0},{4,2},{6,4},{8,6},{10,8},{12,10},{14,12},{3,1},{5,3},{7,5},{... | collective-permute-start | bytes 294920 | tf_op jit(solution)/shard_map/ppermute | solution.py:19
  122.7 6.8 %collective-permute-start = (bf16[2,1,64,384]{3,2,0,1:T(8,128)(2,1)S(1)}, bf16[2,1,64,384]{3,2,0,1:T(8,128)(2,1)S(1)}, u32[]{:S(2)}, u32[]{:S(2)}) collective-permute-start(bf16[2,1,64,384]{3,2,0,1:T(8,128)(2,1)S(1)} %bitcast.126), channel_id=1, source_target_pairs={{0,2},{2,4},{4,6},{6,8},{8,10},{10,12},{12,14},{1,3},{3,5},{5,7},{... | collective-permute-start | bytes 294920 | tf_op jit(solution)/shard_map/ppermute | solution.py:18
  129.5 9.4 %collective-permute-start.2 = (bf16[2,3,64,384]{3,2,0,1:T(8,128)(2,1)S(1)}, bf16[2,3,64,384]{3,2,0,1:T(8,128)(2,1)S(1)}, u32[]{:S(2)}, u32[]{:S(2)}) collective-permute-start(bf16[2,3,64,384]{3,2,0,1:T(8,128)(2,1)S(1)} %pad_maximum_fusion.2), channel_id=1, source_target_pairs={{16,0},{17,1},{18,2},{19,3},{20,4},{21,5},{22,6},{23,7},{24,8},{25... | collective-permute-start | bytes 884744 | tf_op jit(solution)/shard_map/ppermute | solution.py:27
  155.5 12.9 %copy-start.9 = (bf16[1,128,384]{1,2,0:T(8,128)(2,1)S(1)}, bf16[1,128,384]{1,2,0:T(8,128)(2,1)}, u32[]{:S(2)}) copy-start(bf16[1,128,384]{1,2,0:T(8,128)(2,1)} %copy.90) | copy-start | bytes 294916
  155.5 12.9 %copy-start.8 = (bf16[1,128,384]{1,2,0:T(8,128)(2,1)S(1)}, bf16[1,128,384]{1,2,0:T(8,128)(2,1)}, u32[]{:S(2)}) copy-start(bf16[1,128,384]{1,2,0:T(8,128)(2,1)} %copy.91) | copy-start | bytes 294916
  155.5 12.9 %copy-start.4 = (bf16[1,128,384]{1,2,0:T(8,128)(2,1)S(1)}, bf16[1,128,384]{1,2,0:T(8,128)(2,1)}, u32[]{:S(2)}) copy-start(bf16[1,128,384]{1,2,0:T(8,128)(2,1)} %copy.92) | copy-start | bytes 294916
  155.5 13.0 %copy-start.7 = (bf16[1,128,384]{1,2,0:T(8,128)(2,1)S(1)}, bf16[1,128,384]{1,2,0:T(8,128)(2,1)}, u32[]{:S(2)}) copy-start(bf16[1,128,384]{1,2,0:T(8,128)(2,1)} %copy.93) | copy-start | bytes 294916
  155.5 13.0 %copy-start.6 = (bf16[1,128,384]{1,2,0:T(8,128)(2,1)S(1)}, bf16[1,128,384]{1,2,0:T(8,128)(2,1)}, u32[]{:S(2)}) copy-start(bf16[1,128,384]{1,2,0:T(8,128)(2,1)} %copy.94) | copy-start | bytes 294916
  155.5 13.0 %copy-start.5 = (bf16[1,128,384]{1,2,0:T(8,128)(2,1)S(1)}, bf16[1,128,384]{1,2,0:T(8,128)(2,1)}, u32[]{:S(2)}) copy-start(bf16[1,128,384]{1,2,0:T(8,128)(2,1)} %copy.96) | copy-start | bytes 294916
  155.6 13.1 %copy-start.3 = (bf16[1,128,384]{1,2,0:T(8,128)(2,1)S(1)}, bf16[1,128,384]{1,2,0:T(8,128)(2,1)}, u32[]{:S(2)}) copy-start(bf16[1,128,384]{1,2,0:T(8,128)(2,1)} %copy.97) | copy-start | bytes 294916
  155.6 13.2 %copy-start.13 = (bf16[1,2,1,64,384]{4,3,2,1,0:T(8,128)(2,1)S(1)}, bf16[1,2,1,64,384]{4,3,2,1,0:T(8,128)(2,1)}, u32[]{:S(2)}) copy-start(bf16[1,2,1,64,384]{4,3,2,1,0:T(8,128)(2,1)} %param.7) | copy-start | bytes 294916
  186.0 202.4 %all-reduce.3.cloned.1.call-start = ((), (), s32[]{:S(2)}) async-start(), calls=%async_computation.4 | async-start | bytes 2359296 | tf_op jit(solution)/shard_map/psum | solution.py:113
Sparse Core Ops, SparseCore 0:
  53.9 65.8 reduce-scatter.2
  186.1 163.2 reduce-scatter.4
  351.9 36.3 all-reduce.2
where the time goes:
time: 399 us; the launch traced here: 398 us
  waiting for transfers between devices  266 us (67%)
  local copies, waits for them, and re-layouts  51.5 us (13%)
  blocking collectives  33.8 us (8%)
  matrix products  20.9 us (5%)
  between operations  14.2 us (4%)
  starting transfers between devices  7.26 us (2%)
  other arithmetic  4.15 us (1%)
    reduce_scatter x1, waiting for transfers between devices, local(): lax.psum_scatter(term.astype(jnp.bfloat16), 'height', scatter_dimension=0...  160 us
    reduce_scatter x1, waiting for transfers between devices, local(): lax.psum_scatter(jnp.concatenate([grad_k, grad_v], -1).reshape(local_pos...  64.2 us
    all_gather x1, blocking collectives, local(): all_normed = lax.all_gather(normed_rows, 'height', axis=1, tiled=True)  33.8 us
    psum x1, waiting for transfers between devices, local(): weight_grad = lax.psum(banded, ('tm', 'batch')).astype(jnp.float32)  31.8 us
    another operation x28, local copies, waits for them, and re-layouts, local(): stacked = jnp.stack(windows, 0)  16.5 us
    unnamed x57, local copies, waits for them, and re-layouts  15.9 us
    convert_element_type x1, local copies, waits for them, and re-layouts, local(): term.astype(jnp.bfloat16)  12.9 us
  transfers between devices with their start and end apart: 6, of which 6 were waited for; matrix products, arithmetic and copies ran while one was open for 3% of the time, Pallas kernels for 0%

commit v1 on v0

v1 whole, which is shorter than its diff:
```python
import functools
import math

import jax
import jax.numpy as jnp
from jax import lax
from jax.experimental import pallas as pl
from jax.experimental.pallas import tpu as pltpu
from jax.sharding import PartitionSpec as P

EPS = 1e-06
NT = (((1,), (1,)), ((), ()))
TN = (((0,), (0,)), ((), ()))
F32 = jnp.float32
BF16 = jnp.bfloat16


def mm(x, y):
    return jnp.dot(x, y, preferred_element_type=F32)


def mm_nt(x, y):
    return lax.dot_general(x, y, NT, preferred_element_type=F32)


def mm_tn(x, y):
    return lax.dot_general(x, y, TN, preferred_element_type=F32)


def body(
    sizes,
    saved_ref, cot_ref, conv_ref, gain_ref, wqkv_hbm, wout_hbm, wconv_hbm,
    igrad_ref, wgrad_ref,
    wqkv, wout, wconv, xall, conv_t, recv_t, gpad, lhs, win,
    part_f, part_b, half_f, half_b, got1, got2, total, ig_send, ig_got,
    wsem, gs_sem, gr_sem, cs_sem, cr_sem, is_sem, ir_sem,
    s1s, s1r, s2s, s2r, s3s, s3r, s4s, s4r,
):
    n_t, n_h, n_b, frames, columns, chans, tp = sizes
    tile = frames * columns
    dblk = chans // n_h
    n_a = n_h // 2
    ht = n_t * tp
    t = lax.axis_index("tm")
    h = lax.axis_index("height")
    c = lax.axis_index("batch")
    scale = 1.0 / math.sqrt(chans)
    norm = 1.0 / math.sqrt(n_b * n_t * frames * n_h * columns)

    loads = [
        pltpu.make_async_copy(wqkv_hbm, wqkv, wsem.at[0]),
        pltpu.make_async_copy(wout_hbm, wout, wsem.at[1]),
        pltpu.make_async_copy(wconv_hbm, wconv, wsem.at[2]),
    ]
    for load in loads:
        load.start()

    def remote(src, dst, ssem, rsem, dev):
        return pltpu.make_async_remote_copy(
            src_ref=src, dst_ref=dst, send_sem=ssem, recv_sem=rsem,
            device_id=dev, device_id_type=pl.DeviceIdType.MESH,
        )

    barrier = pltpu.get_barrier_semaphore()
    for dt in range(n_t):
        for dh in range(n_h):
            if dt or dh:
                pl.semaphore_signal(
                    barrier, inc=1,
                    device_id=(lax.rem(t + dt, n_t), lax.rem(h + dh, n_h), c),
                    device_id_type=pl.DeviceIdType.MESH,
                )
    for db in range(1, n_b):
        pl.semaphore_signal(
            barrier, inc=1, device_id=(t, h, lax.rem(c + db, n_b)),
            device_id_type=pl.DeviceIdType.MESH,
        )
    pl.semaphore_wait(barrier, n_t * n_h - 1 + n_b - 1)

    h_a, h_b = h // 2, lax.rem(h, 2)
    mate = h_a * 2 + (1 - h_b)
    order = sorted(range(1, n_a), key=lambda k: min(k, n_a - k))
    sends = []
    mine = (saved_ref, cot_ref)
    for arr in range(2):
        for k in order:
            peer = lax.rem(h_a + k, n_a) * 2 + h_b
            cp = remote(mine[arr], xall.at[arr, h], gs_sem.at[arr, k], gr_sem.at[arr, h], (t, peer, c))
            cp.start()
            sends.append(cp)
        cp = remote(mine[arr], xall.at[arr, h], gs_sem.at[arr, 0], gr_sem.at[arr, h], (t, mate, c))
        cp.start()
        sends.append(cp)
    for arr in range(2):
        xall[arr, h] = mine[arr][...]

    flipped = conv_ref[...].astype(F32).T.astype(BF16)
    for k in range(n_h):
        conv_t[k] = flipped[k * dblk:(k + 1) * dblk]
    recv_t[0, h] = conv_t[h]

    for arr in range(2):
        for k in order:
            src = lax.rem(h_a + k, n_a) * 2 + h_b
            remote(mine[arr], xall.at[arr, src], gs_sem.at[arr, k], gr_sem.at[arr, src], (t, mate, c)).wait_recv()
            cp = remote(xall.at[arr, src], xall.at[arr, src], gs_sem.at[arr, n_a + k - 1], gr_sem.at[arr, src], (t, mate, c))
            cp.start()
            sends.append(cp)

    for k in range(1, n_h):
        peer = lax.rem(h + k, n_h)
        cp = remote(conv_t.at[peer], recv_t.at[0, h], cs_sem.at[0, k], cr_sem.at[0, h], (t, peer, c))
        cp.start()
        sends.append(cp)

    def to_next(k):
        peer = lax.rem(h + k, n_h)
        later = jnp.minimum(t + 1, n_t - 1)
        return remote(conv_t.at[peer], recv_t.at[1, h], cs_sem.at[1, k], cr_sem.at[1, h], (later, peer, c))

    @pl.when(t < n_t - 1)
    def _():
        for k in range(n_h):
            to_next(k).start()

    @pl.when(t == 0)
    def _():
        recv_t[1] = jnp.zeros_like(recv_t[1])

    for arr in range(2):
        for k in range(n_a):
            src = lax.rem(h_a + k, n_a) * 2 + (1 - h_b)
            remote(mine[arr], xall.at[arr, src], gs_sem.at[arr, 0], gr_sem.at[arr, src], (t, mate, c)).wait_recv()

    loads[0].wait()
    loads[1].wait()
    gain = gain_ref[...]
    keys_n = n_h * columns
    gpad[0] = jnp.zeros_like(gpad[0])
    gpad[n_h + 1] = jnp.zeros_like(gpad[0])

    def frame(f, carry):
        rows = pl.ds(pl.multiple_of(f * columns, columns), columns)
        hidden = xall[0, :, rows, :].reshape(keys_n, chans).astype(F32)
        cot = xall[1, :, rows, :].reshape(keys_n, chans)
        inverse = lax.rsqrt(jnp.mean(hidden * hidden, -1, keepdims=True) + EPS)
        normed = (hidden * inverse * gain).astype(BF16)
        qkv = mm(normed, wqkv[...]).astype(BF16)
        q, k, v = qkv[:, :chans], qkv[:, chans:2 * chans], qkv[:, 2 * chans:]
        go = mm_nt(cot, wout[...]).astype(BF16)
        s = mm_nt(k, q) * scale
        e = jnp.exp(s - jnp.max(s, 0, keepdims=True))
        p = e / jnp.sum(e, 0, keepdims=True)
        gp = mm_nt(v, go)
        delta = jnp.sum(p * gp, 0, keepdims=True)
        gs = (p * (gp - delta) * scale).astype(BF16)
        gq = mm_tn(gs, k).astype(BF16)
        gk = mm(gs, q).astype(BF16)
        gv = mm(p.astype(BF16), go).astype(BF16)
        gn = (
            mm_nt(gq, wqkv[:, :chans])
            + mm_nt(gk, wqkv[:, chans:2 * chans])
            + mm_nt(gv, wqkv[:, 2 * chans:])
        )
        scaled = gn * gain
        g = cot.astype(F32) + inverse * (
            scaled - hidden * inverse * inverse * jnp.mean(scaled * hidden, -1, keepdims=True)
        )
        gpad[1:n_h + 1, rows, :] = g.astype(BF16).reshape(n_h, columns, chans)
        return carry

    lax.fori_loop(0, frames, frame, 0)

    for k in range(1, n_h):
        src = lax.rem(h + k, n_h)
        remote(conv_t.at[0], recv_t.at[0, src], cs_sem.at[0, k], cr_sem.at[0, src], (t, src, c)).wait_recv()

    @pl.when(t > 0)
    def _():
        for k in range(n_h):
            src = lax.rem(h + k, n_h)
            remote(conv_t.at[0], recv_t.at[1, src], cs_sem.at[1, k], cr_sem.at[1, src], (t, mate, c)).wait_recv()

    lane = lax.broadcasted_iota(jnp.int32, (dblk, tile), 1)
    for a in range(3):
        for j in range(3):
            lhs[3 * a + j, 0] = jnp.zeros((dblk, tile), BF16)
            lhs[3 * a + j, n_h + 1] = jnp.zeros((dblk, tile), BF16)

    def shifts(r, carry):
        own = recv_t[0, r].astype(F32)
        prev = recv_t[1, r].astype(F32)
        both = jnp.where(lane < columns, pltpu.roll(prev, columns, 1), pltpu.roll(own, columns, 1))
        for a, x in enumerate((prev, both, own)):
            left = jnp.where(lax.rem(lane, columns) == 0, 0.0, pltpu.roll(x, 1, 1))
            right = jnp.where(lax.rem(lane, columns) == columns - 1, 0.0, pltpu.roll(x, tile - 1, 1))
            for j, y in enumerate((left, x, right)):
                lhs[3 * a + j, r + 1] = y.astype(BF16)
        return carry

    lax.fori_loop(0, n_h, shifts, 0)

    for b in range(3):
        rights = gpad[1:n_h + 1].reshape(n_h * tile, chans)
        left = jnp.concatenate(
            [lhs[:, b + r].reshape(9 * dblk, tile) for r in range(n_h)], axis=1
        )
        out = (mm(left, rights) * norm).reshape(9, dblk, chans)
        for a in range(3):
            for j in range(3):
                tap = 9 * a + 3 * b + j
                part_f[tap] = out[3 * a + j]
                part_b[tap] = out[3 * a + j].astype(BF16)
    for tap in range(27, n_b * ht):
        part_f[tap] = jnp.zeros((dblk, chans), F32)
        part_b[tap] = jnp.zeros((dblk, chans), BF16)

    for k in range(1, n_b):
        peer = lax.rem(c + k, n_b)
        cp = remote(part_b.at[pl.ds(peer * ht, ht)], got1.at[c], s1s.at[k], s1r.at[c], (t, h, peer))
        cp.start()
        sends.append(cp)

    row = lax.broadcasted_iota(jnp.int32, (tile, chans), 0)
    for b in range(3):
        x = gpad[h + 2 - b].astype(F32)
        ahead = jnp.where(lax.rem(row, columns) == columns - 1, 0.0, pltpu.roll(x, tile - 1, 0))
        behind = jnp.where(lax.rem(row, columns) == 0, 0.0, pltpu.roll(x, 1, 0))
        for j, y in enumerate((ahead, x, behind)):
            win[3 * b + j] = y.astype(BF16)
    loads[2].wait()

    def taps(a):
        acc = mm_nt(win[0], wconv[9 * a])
        for i in range(1, 9):
            acc = acc + mm_nt(win[i], wconv[9 * a + i])
        return acc

    y0, y1 = taps(0), taps(1)
    cut = columns
    ig_send[...] = jnp.concatenate([y0[:cut], y0[cut:] + y1[:cut]], 0).astype(BF16)

    def to_prev():
        return remote(ig_send, ig_got, is_sem, ir_sem, (jnp.maximum(t - 1, 0), h, c))

    @pl.when(t > 0)
    def _():
        to_prev().start()

    @pl.when(t == n_t - 1)
    def _():
        ig_got[...] = jnp.zeros_like(ig_got)

    acc = part_f[pl.ds(c * ht, ht)]
    for k in range(1, n_b):
        peer = lax.rem(c + k, n_b)
        remote(part_b.at[pl.ds(0, ht)], got1.at[peer], s1s.at[k], s1r.at[peer], (t, h, peer)).wait_recv()
        acc = acc + got1[peer].astype(F32)
    half_f[...] = acc
    half_b[...] = acc.astype(BF16)
    for k in range(1, n_t):
        peer = lax.rem(t + k, n_t)
        cp = remote(half_b.at[pl.ds(peer * tp, tp)], got2.at[t], s2s.at[k], s2r.at[t], (peer, h, c))
        cp.start()
        sends.append(cp)

    y2 = taps(2)
    own_ig = y2 + jnp.concatenate([y1[cut:], jnp.zeros((tile - cut, chans), F32)], 0)

    acc = half_f[pl.ds(t * tp, tp)]
    for k in range(1, n_t):
        peer = lax.rem(t + k, n_t)
        remote(half_b.at[pl.ds(0, tp)], got2.at[peer], s2s.at[k], s2r.at[peer], (peer, h, c)).wait_recv()
        acc = acc + got2[peer].astype(F32)
    total[c, t] = acc.astype(BF16)

    for k in range(1, n_t):
        peer = lax.rem(t + k, n_t)
        cp = remote(total.at[c, t], total.at[c, t], s3s.at[k], s3r.at[t], (peer, h, c))
        cp.start()
        sends.append(cp)

    def across(piece, k):
        return remote(
            total.at[c, piece], total.at[c, piece], s4s.at[piece, k], s4r.at[c, piece],
            (t, h, lax.rem(c + k, n_b)),
        )

    for k in range(1, n_b):
        cp = across(t, k)
        cp.start()
        sends.append(cp)

    @pl.when(t < n_t - 1)
    def _():
        to_prev().wait_recv()

    igrad_ref[...] = (own_ig + ig_got[...].astype(F32)).astype(BF16)

    for m in range(1, n_t):
        peer = lax.rem(t + m, n_t)
        remote(total.at[c, peer], total.at[c, peer], s3s.at[m], s3r.at[peer], (peer, h, c)).wait_recv()
        for k in range(1, n_b):
            cp = across(peer, k)
            cp.start()
            sends.append(cp)
    for m in range(n_t):
        piece = lax.rem(t + m, n_t)
        for k in range(1, n_b):
            peer = lax.rem(c + k, n_b)
            remote(
                total.at[peer, piece], total.at[peer, piece], s4s.at[piece, k], s4r.at[peer, piece],
                (t, h, peer),
            ).wait_recv()
    wgrad_ref[...] = total[...].reshape(n_b * ht, dblk, chans)

    for cp in sends:
        cp.wait_send()

    @pl.when(t < n_t - 1)
    def _():
        for k in range(n_h):
            to_next(k).wait_send()

    @pl.when(t > 0)
    def _():
        to_prev().wait_send()


def local(conv_input, saved, cotangent, gain, w_conv, w_qkv, w_out):
    chans = saved.shape[-1]
    frames, columns = saved.shape[1], saved.shape[2] * saved.shape[3]
    n_t, n_h, n_b = (lax.axis_size(x) for x in ("tm", "height", "batch"))
    tile = frames * columns
    dblk = chans // n_h
    tp = -(-27 // (n_t * n_b))
    ht = n_t * tp
    taps = n_b * ht
    sizes = (n_t, n_h, n_b, frames, columns, chans, tp)
    vmem = pl.BlockSpec(memory_space=pltpu.VMEM)
    hbm = pl.BlockSpec(memory_space=pl.ANY)
    dma = pltpu.SemaphoreType.DMA
    igrad, wgrad = pl.pallas_call(
        functools.partial(body, sizes),
        out_shape=(
            jax.ShapeDtypeStruct((tile, chans), BF16),
            jax.ShapeDtypeStruct((taps, dblk, chans), BF16),
        ),
        in_specs=[vmem] * 4 + [hbm] * 3,
        out_specs=(vmem, vmem),
        scratch_shapes=[
            pltpu.VMEM((chans, 3 * chans), BF16),
            pltpu.VMEM((chans, chans), BF16),
            pltpu.VMEM((27, chans, chans), BF16),
            pltpu.VMEM((2, n_h, tile, chans), BF16),
            pltpu.VMEM((n_h, dblk, tile), BF16),
            pltpu.VMEM((2, n_h, dblk, tile), BF16),
            pltpu.VMEM((n_h + 2, tile, chans), BF16),
            pltpu.VMEM((9, n_h + 2, dblk, tile), BF16),
            pltpu.VMEM((9, tile, chans), BF16),
            pltpu.VMEM((taps, dblk, chans), F32),
            pltpu.VMEM((taps, dblk, chans), BF16),
            pltpu.VMEM((ht, dblk, chans), F32),
            pltpu.VMEM((ht, dblk, chans), BF16),
            pltpu.VMEM((n_b, ht, dblk, chans), BF16),
            pltpu.VMEM((n_t, tp, dblk, chans), BF16),
            pltpu.VMEM((n_b, n_t, tp, dblk, chans), BF16),
            pltpu.VMEM((tile, chans), BF16),
            pltpu.VMEM((tile, chans), BF16),
            dma((3,)), dma((2, n_h)), dma((2, n_h)), dma((2, n_h)), dma((2, n_h)), dma, dma,
            dma((n_b,)), dma((n_b,)), dma((n_t,)), dma((n_t,)), dma((n_t,)), dma((n_t,)),
            dma((n_t, n_b)), dma((n_b, n_t)),
        ],
        compiler_params=pltpu.CompilerParams(
            collective_id=0, has_side_effects=True, vmem_limit_bytes=56 * 1024 * 1024
        ),
    )(
        saved.reshape(tile, chans), cotangent.reshape(tile, chans), conv_input.reshape(tile, chans),
        gain.reshape(1, chans), w_qkv, w_out, w_conv.reshape(27, chans, chans),
    )
    weight_grad = wgrad[:27].astype(F32).transpose(1, 0, 2)
    return igrad.reshape(conv_input.shape), weight_grad


def solution(mesh):
    banded = P("batch", "tm", "height", None, None)
    return jax.shard_map(
        local,
        mesh=mesh,
        in_specs=(banded, banded, banded, P(), P(), P(), P()),
        out_specs=(banded, P("height", None, None)),
        check_vma=False,
    )
```

time: 399 us -> 67.1 us (0.17)
  waiting for transfers between devices: 266 us -> 0 us
  Pallas kernels: 0 us -> 60.9 us
  local copies, waits for them, and re-layouts: 51.5 us -> 1.89 us
  blocking collectives: 33.8 us -> 0 us
  matrix products: 20.9 us -> 0 us
  between operations: 14.2 us -> 0.65 us
  starting transfers between devices: 7.26 us -> 0 us
    reduce_scatter x2 -> x0, waiting for transfers between devices: 224 us -> none  [the longest x1 160 us: local(): lax.psum_scatter(term.astype(jnp.bfloat16), 'height', scatter_dimension=0...]
    pallas_call x0 -> x1, Pallas kernels: none -> 60.9 us  [local(): pl.pallas_call(functools.partial(body, sizes), out_shape=(jax.ShapeDtypeS...]
    all_gather x1 -> x0, blocking collectives: 33.8 us -> none  [local(): all_normed = lax.all_gather(normed_rows, 'height', axis=1, tiled=True)]
    psum x1 -> x0, waiting for transfers between devices: 31.8 us -> none  [local(): weight_grad = lax.psum(banded, ('tm', 'batch')).astype(jnp.float32)]
    dot_general x11 -> x0, matrix products: 20.9 us -> none  [the longest x1 7.11 us: local(): jnp.einsum('trc,tdc->rd', stacked, kernel, preferred_element_type=jnp.flo...]
    another operation x28 -> x0, local copies, waits for them, and re-layouts: 16.5 us -> none  [local(): stacked = jnp.stack(windows, 0)]
    convert_element_type x3 -> x0, local copies, waits for them, and re-layouts: 15.4 us -> none  [the longest x1 12.9 us: local(): term.astype(jnp.bfloat16)]
    unnamed x57 -> x3, local copies, waits for them, and re-layouts: 15.9 us -> 0.64 us
  transfers between devices with their start and end apart: 6 -> 0, of which waited for: 6 -> 0; matrix products, arithmetic and copies ran while one was open for 3% -> 0% of each run, Pallas kernels for 0% -> 0%
where the time goes in v1:
time: 67.1 us; the launch traced here: 66.1 us
  Pallas kernels  60.9 us (91%)
  other arithmetic  2.65 us (4%)
  local copies, waits for them, and re-layouts  1.89 us (3%)
    pallas_call x1, Pallas kernels, local(): pl.pallas_call(functools.partial(body, sizes), out_shape=(jax.ShapeDtypeS...  60.9 us
    transpose x1, other arithmetic, local(): weight_grad = wgrad[:27].astype(F32).transpose(1, 0, 2)  2.65 us

profile of v1, /device:TPU:0, one launch (start us, length us, event | category | flops | bytes accessed | tf_op | source)
XLA Modules:
  0.0 66.1 jit_solution(1864099822584626358)
XLA Ops:
  0.6 1.2 %reshape.25.gain_ref = f32[1,384]{1,0:T(1,128)} reshape(f32[384]{0:T(512)} %param.10) | data formatting | bytes 3072 | tf_op jit(solution)/shard_map/reshape | solution.py:379
  1.9 60.9 %shard_map.86 = (bf16[128,384]{1,0:T(8,128)(2,1)}, bf16[28,48,384]{2,1,0:T(8,128)(2,1)}) custom-call(bf16[128,384]{1,0:T(8,128)(2,1)} %bitcast.10, bf16[128,384]{1,0:T(8,128)(2,1)} %bitcast.11, bf16[128,384]{1,0:T(8,128)(2,1)} %bitcast.12, f32[1,384]{1,0:T(1,128)} %reshape.25.gain_ref, bf16[384,1152]{1,0:T(8,128)(2,1)} %wqkv_hbm.1, ...), custom_call_target="tpu_custom_call" | custom-call | tf_op jit(solution)/shard_map/pallas_call | solution.py:343
  62.8 0.0 copy-start
  62.8 2.6 %convert_bitcast_fusion = f32[48,27,384]{2,0,1:T(8,128)} fusion(bf16[28,48,384]{2,1,0:T(8,128)(2,1)} %get-tuple-element.5), kind=kLoop, calls=%fused_computation | loop fusion | flops 497664 | bytes 2985984 | tf_op jit(solution)/shard_map/transpose | solution.py:381
  65.4 0.0 copy-done
  65.4 0.6 copy.11
Async XLA Ops:
  62.8 2.7 %copy-start = (bf16[128,384]{1,0:T(8,128)(2,1)S(1)}, bf16[128,384]{1,0:T(8,128)(2,1)}, u32[]{:S(2)}) copy-start(bf16[128,384]{1,0:T(8,128)(2,1)} %get-tuple-element.4) | copy-start | bytes 294916

commit v2 on v1

--- a/solution.py
+++ b/solution.py
@@ -82,15 +82,38 @@
     order = sorted(range(1, n_a), key=lambda k: min(k, n_a - k))
     sends = []
     mine = (saved_ref, cot_ref)
-    for arr in range(2):
-        for k in order:
-            peer = lax.rem(h_a + k, n_a) * 2 + h_b
-            cp = remote(mine[arr], xall.at[arr, h], gs_sem.at[arr, k], gr_sem.at[arr, h], (t, peer, c))
+
+    def block(f, arr, src, slot, dev, own=False):
+        rows = pl.ds(f * columns, columns)
+        dst = xall.at[arr, src, rows]
+        return remote(
+            mine[arr].at[rows] if own else dst, dst,
+            gs_sem.at[2 * f + arr, slot], gr_sem.at[2 * f + arr, src], (t, dev, c),
+        )
+
+    def send_own(f):
+        for arr in range(2):
+            for k in order:
+                cp = block(f, arr, h, k, lax.rem(h_a + k, n_a) * 2 + h_b, True)
+                cp.start()
+                sends.append(cp)
+            cp = block(f, arr, h, 0, mate, True)
             cp.start()
             sends.append(cp)
-        cp = remote(mine[arr], xall.at[arr, h], gs_sem.at[arr, 0], gr_sem.at[arr, h], (t, mate, c))
+
+    def pass_on(f, arr, k):
+        src = lax.rem(h_a + k, n_a) * 2 + h_b
+        block(f, arr, src, k, mate).wait_recv()
+        cp = block(f, arr, src, n_a + k - 1, mate)
         cp.start()
         sends.append(cp)
+
+    def arrived(f, arr):
+        for k in range(n_a):
+            src = lax.rem(h_a + k, n_a) * 2 + (1 - h_b)
+            block(f, arr, src, 0, mate).wait_recv()
+
+    send_own(0)
     for arr in range(2):
         xall[arr, h] = mine[arr][...]
 
@@ -101,11 +124,9 @@
 
     for arr in range(2):
         for k in order:
-            src = lax.rem(h_a + k, n_a) * 2 + h_b
-            remote(mine[arr], xall.at[arr, src], gs_sem.at[arr, k], gr_sem.at[arr, src], (t, mate, c)).wait_recv()
-            cp = remote(xall.at[arr, src], xall.at[arr, src], gs_sem.at[arr, n_a + k - 1], gr_sem.at[arr, src], (t, mate, c))
-            cp.start()
-            sends.append(cp)
+            pass_on(0, arr, k)
+    for f in range(1, frames):
+        send_own(f)
 
     for k in range(1, n_h):
         peer = lax.rem(h + k, n_h)
@@ -126,11 +147,6 @@
     @pl.when(t == 0)
     def _():
         recv_t[1] = jnp.zeros_like(recv_t[1])
-
-    for arr in range(2):
-        for k in range(n_a):
-            src = lax.rem(h_a + k, n_a) * 2 + (1 - h_b)
-            remote(mine[arr], xall.at[arr, src], gs_sem.at[arr, 0], gr_sem.at[arr, src], (t, mate, c)).wait_recv()
 
     loads[0].wait()
     loads[1].wait()
@@ -139,24 +155,31 @@
     gpad[0] = jnp.zeros_like(gpad[0])
     gpad[n_h + 1] = jnp.zeros_like(gpad[0])
 
-    def frame(f, carry):
-        rows = pl.ds(pl.multiple_of(f * columns, columns), columns)
+    for f in range(frames):
+        rows = pl.ds(f * columns, columns)
+        coming = [(f + 1, arr, k) for arr in range(2) for k in order] if f + 1 < frames else []
+        arrived(f, 0)
         hidden = xall[0, :, rows, :].reshape(keys_n, chans).astype(F32)
-        cot = xall[1, :, rows, :].reshape(keys_n, chans)
         inverse = lax.rsqrt(jnp.mean(hidden * hidden, -1, keepdims=True) + EPS)
         normed = (hidden * inverse * gain).astype(BF16)
         qkv = mm(normed, wqkv[...]).astype(BF16)
         q, k, v = qkv[:, :chans], qkv[:, chans:2 * chans], qkv[:, 2 * chans:]
-        go = mm_nt(cot, wout[...]).astype(BF16)
         s = mm_nt(k, q) * scale
         e = jnp.exp(s - jnp.max(s, 0, keepdims=True))
         p = e / jnp.sum(e, 0, keepdims=True)
+        arrived(f, 1)
+        for item in coming[:len(order) // 2]:
+            pass_on(*item)
+        cot = xall[1, :, rows, :].reshape(keys_n, chans)
+        go = mm_nt(cot, wout[...]).astype(BF16)
         gp = mm_nt(v, go)
         delta = jnp.sum(p * gp, 0, keepdims=True)
         gs = (p * (gp - delta) * scale).astype(BF16)
         gq = mm_tn(gs, k).astype(BF16)
         gk = mm(gs, q).astype(BF16)
         gv = mm(p.astype(BF16), go).astype(BF16)
+        for item in coming[len(order) // 2:len(order)]:
+            pass_on(*item)
         gn = (
             mm_nt(gq, wqkv[:, :chans])
             + mm_nt(gk, wqkv[:, chans:2 * chans])
@@ -167,9 +190,8 @@
             scaled - hidden * inverse * inverse * jnp.mean(scaled * hidden, -1, keepdims=True)
         )
         gpad[1:n_h + 1, rows, :] = g.astype(BF16).reshape(n_h, columns, chans)
-        return carry
-
-    lax.fori_loop(0, frames, frame, 0)
+        for item in coming[len(order):]:
+            pass_on(*item)
 
     for k in range(1, n_h):
         src = lax.rem(h + k, n_h)
@@ -200,26 +222,29 @@
 
     lax.fori_loop(0, n_h, shifts, 0)
 
-    for b in range(3):
-        rights = gpad[1:n_h + 1].reshape(n_h * tile, chans)
-        left = jnp.concatenate(
-            [lhs[:, b + r].reshape(9 * dblk, tile) for r in range(n_h)], axis=1
-        )
-        out = (mm(left, rights) * norm).reshape(9, dblk, chans)
-        for a in range(3):
-            for j in range(3):
-                tap = 9 * a + 3 * b + j
-                part_f[tap] = out[3 * a + j]
-                part_b[tap] = out[3 * a + j].astype(BF16)
     for tap in range(27, n_b * ht):
         part_f[tap] = jnp.zeros((dblk, chans), F32)
         part_b[tap] = jnp.zeros((dblk, chans), BF16)
-
-    for k in range(1, n_b):
-        peer = lax.rem(c + k, n_b)
-        cp = remote(part_b.at[pl.ds(peer * ht, ht)], got1.at[c], s1s.at[k], s1r.at[c], (t, h, peer))
-        cp.start()
-        sends.append(cp)
+    rights = gpad[1:n_h + 1].reshape(n_h * tile, chans)
+    halves = [
+        remote(
+            part_b.at[pl.ds(lax.rem(c + k, n_b) * ht, ht)], got1.at[c], s1s.at[k], s1r.at[c],
+            (t, h, lax.rem(c + k, n_b)),
+        )
+        for k in range(1, n_b)
+    ]
+    sends += halves
+    for i in range(3):
+        b = jnp.where(c == 0, 2 - i, i)
+        left = jnp.concatenate(
+            [lhs[:, b + r].reshape(9 * dblk, tile) for r in range(n_h)], axis=1
+        )
+        out = (mm(left, rights) * norm).reshape(9, dblk, chans)
+        part_f[pl.ds(9 * b, 9)] = out
+        part_b[pl.ds(9 * b, 9)] = out.astype(BF16)
+        if i == (1 if n_b == 2 and ht <= 18 else 2):
+            for cp in halves:
+                cp.start()
 
     row = lax.broadcasted_iota(jnp.int32, (tile, chans), 0)
     for b in range(3):
@@ -236,21 +261,7 @@
             acc = acc + mm_nt(win[i], wconv[9 * a + i])
         return acc
 
-    y0, y1 = taps(0), taps(1)
-    cut = columns
-    ig_send[...] = jnp.concatenate([y0[:cut], y0[cut:] + y1[:cut]], 0).astype(BF16)
-
-    def to_prev():
-        return remote(ig_send, ig_got, is_sem, ir_sem, (jnp.maximum(t - 1, 0), h, c))
-
-    @pl.when(t > 0)
-    def _():
-        to_prev().start()
-
-    @pl.when(t == n_t - 1)
-    def _():
-        ig_got[...] = jnp.zeros_like(ig_got)
-
+    y0 = taps(0)
     acc = part_f[pl.ds(c * ht, ht)]
     for k in range(1, n_b):
         peer = lax.rem(c + k, n_b)
@@ -263,6 +274,21 @@
         cp = remote(half_b.at[pl.ds(peer * tp, tp)], got2.at[t], s2s.at[k], s2r.at[t], (peer, h, c))
         cp.start()
         sends.append(cp)
+
+    y1 = taps(1)
+    cut = columns
+    ig_send[...] = jnp.concatenate([y0[:cut], y0[cut:] + y1[:cut]], 0).astype(BF16)
+
+    def to_prev():
+        return remote(ig_send, ig_got, is_sem, ir_sem, (jnp.maximum(t - 1, 0), h, c))
+
+    @pl.when(t > 0)
+    def _():
+        to_prev().start()
+
+    @pl.when(t == n_t - 1)
+    def _():
+        ig_got[...] = jnp.zeros_like(ig_got)
 
     y2 = taps(2)
     own_ig = y2 + jnp.concatenate([y1[cut:], jnp.zeros((tile - cut, chans), F32)], 0)
@@ -312,7 +338,10 @@
                 total.at[peer, piece], total.at[peer, piece], s4s.at[piece, k], s4r.at[peer, piece],
                 (t, h, peer),
             ).wait_recv()
-    wgrad_ref[...] = total[...].reshape(n_b * ht, dblk, chans)
+    whole = total.reshape(n_b * ht, dblk, chans)
+    for a in range(3):
+        for b in range(3):
+            wgrad_ref[9 * a + 3 * b:9 * a + 3 * b + 3] = whole[9 * b + 3 * a:9 * b + 3 * a + 3]
 
     for cp in sends:
         cp.wait_send()
@@ -344,7 +373,7 @@
         functools.partial(body, sizes),
         out_shape=(
             jax.ShapeDtypeStruct((tile, chans), BF16),
-            jax.ShapeDtypeStruct((taps, dblk, chans), BF16),
+            jax.ShapeDtypeStruct((27, dblk, chans), BF16),
         ),
         in_specs=[vmem] * 4 + [hbm] * 3,
         out_specs=(vmem, vmem),
@@ -367,7 +396,7 @@
             pltpu.VMEM((n_b, n_t, tp, dblk, chans), BF16),
             pltpu.VMEM((tile, chans), BF16),
             pltpu.VMEM((tile, chans), BF16),
-            dma((3,)), dma((2, n_h)), dma((2, n_h)), dma((2, n_h)), dma((2, n_h)), dma, dma,
+            dma((3,)), dma((2 * frames, n_h)), dma((2 * frames, n_h)), dma((2, n_h)), dma((2, n_h)), dma, dma,
             dma((n_b,)), dma((n_b,)), dma((n_t,)), dma((n_t,)), dma((n_t,)), dma((n_t,)),
             dma((n_t, n_b)), dma((n_b, n_t)),
         ],
@@ -378,7 +407,7 @@
         saved.reshape(tile, chans), cotangent.reshape(tile, chans), conv_input.reshape(tile, chans),
         gain.reshape(1, chans), w_qkv, w_out, w_conv.reshape(27, chans, chans),
     )
-    weight_grad = wgrad[:27].astype(F32).transpose(1, 0, 2)
+    weight_grad = wgrad.astype(F32).transpose(1, 0, 2)
     return igrad.reshape(conv_input.shape), weight_grad
 
 

time: 67.1 us -> 61.8 us (0.921); the launches traced: 66.1 us -> 61.5 us
  Pallas kernels: 60.9 us -> 56.4 us
    pallas_call x1, Pallas kernels: 60.9 us -> 56.4 us  [local(): pl.pallas_call(functools.partial(body, sizes), out_shape=(jax.ShapeDtypeS...]
where the time goes in v2:
time: 61.8 us; the launch traced here: 61.5 us
  Pallas kernels  56.4 us (91%)
  other arithmetic  2.65 us (4%)
  local copies, waits for them, and re-layouts  1.89 us (3%)
  between operations  0.65 us (1%)
    pallas_call x1, Pallas kernels, local(): pl.pallas_call(functools.partial(body, sizes), out_shape=(jax.ShapeDtypeS...  56.4 us
    transpose x1, other arithmetic, local(): weight_grad = wgrad.astype(F32).transpose(1, 0, 2)  2.65 us
    reshape x1, local copies, waits for them, and re-layouts, local(): gain.reshape(1, chans)  1.25 us

profile of v2, /device:TPU:0, one launch (start us, length us, event | category | flops | bytes accessed | tf_op | source)
XLA Modules:
  0.0 61.5 jit_solution(9536097420555874241)
XLA Ops:
  0.6 1.2 %reshape.25.gain_ref = f32[1,384]{1,0:T(1,128)} reshape(f32[384]{0:T(512)} %param.10) | data formatting | bytes 3072 | tf_op jit(solution)/shard_map/reshape | solution.py:408
  1.9 56.4 %shard_map.86 = (bf16[128,384]{1,0:T(8,128)(2,1)}, bf16[27,48,384]{2,1,0:T(8,128)(2,1)}) custom-call(bf16[128,384]{1,0:T(8,128)(2,1)} %bitcast.10, bf16[128,384]{1,0:T(8,128)(2,1)} %bitcast.11, bf16[128,384]{1,0:T(8,128)(2,1)} %bitcast.12, f32[1,384]{1,0:T(1,128)} %reshape.25.gain_ref, bf16[384,1152]{1,0:T(8,128)(2,1)} %wqkv_hbm.1, ...), custom_call_target="tpu_custom_call" | custom-call | tf_op jit(solution)/shard_map/pallas_call | solution.py:372
  58.2 0.0 copy-start
  58.2 2.6 %convert_bitcast_fusion = f32[48,27,384]{2,0,1:T(8,128)} fusion(bf16[27,48,384]{2,1,0:T(8,128)(2,1)} %get-tuple-element.5), kind=kLoop, calls=%fused_computation | loop fusion | flops 497664 | bytes 2985984 | tf_op jit(solution)/shard_map/transpose | solution.py:410
  60.9 0.0 copy-done
  60.9 0.6 %copy.11 = bf16[1,2,1,64,384]{4,3,2,1,0:T(8,128)(2,1)} copy(bf16[1,2,1,64,384]{4,3,2,1,0:T(8,128)(2,1)S(1)} %bitcast.13) | data formatting | bytes 196608
Async XLA Ops:
  58.2 2.7 %copy-start = (bf16[128,384]{1,0:T(8,128)(2,1)S(1)}, bf16[128,384]{1,0:T(8,128)(2,1)}, u32[]{:S(2)}) copy-start(bf16[128,384]{1,0:T(8,128)(2,1)} %get-tuple-element.4) | copy-start | bytes 294916

commit v3 on v2

--- a/solution.py
+++ b/solution.py
@@ -31,16 +31,15 @@
     sizes,
     saved_ref, cot_ref, conv_ref, gain_ref, wqkv_hbm, wout_hbm, wconv_hbm,
     igrad_ref, wgrad_ref,
-    wqkv, wout, wconv, xall, conv_t, recv_t, gpad, lhs, win,
-    part_f, part_b, half_f, half_b, got1, got2, total, ig_send, ig_got,
-    wsem, gs_sem, gr_sem, cs_sem, cr_sem, is_sem, ir_sem,
-    s1s, s1r, s2s, s2r, s3s, s3r, s4s, s4r,
+    wqkv, wout, wconv, xall, conv_t, recv_t, gpad, gall, lhs, win,
+    part_f, part_b, got1, total, ig_send, ig_got,
+    wsem, gs_sem, gr_sem, cs_sem, cr_sem, xs_sem, xr_sem, is_sem, ir_sem,
+    s1s, s1r, s4s, s4r,
 ):
-    n_t, n_h, n_b, frames, columns, chans, tp = sizes
+    n_t, n_h, n_b, frames, columns, chans, ht = sizes
     tile = frames * columns
     dblk = chans // n_h
     n_a = n_h // 2
-    ht = n_t * tp
     t = lax.axis_index("tm")
     h = lax.axis_index("height")
     c = lax.axis_index("batch")
@@ -120,7 +119,7 @@
     flipped = conv_ref[...].astype(F32).T.astype(BF16)
     for k in range(n_h):
         conv_t[k] = flipped[k * dblk:(k + 1) * dblk]
-    recv_t[0, h] = conv_t[h]
+    recv_t[t, h] = conv_t[h]
 
     for arr in range(2):
         for k in order:
@@ -128,25 +127,36 @@
     for f in range(1, frames):
         send_own(f)
 
-    for k in range(1, n_h):
-        peer = lax.rem(h + k, n_h)
-        cp = remote(conv_t.at[peer], recv_t.at[0, h], cs_sem.at[0, k], cr_sem.at[0, h], (t, peer, c))
-        cp.start()
-        sends.append(cp)
-
-    def to_next(k):
-        peer = lax.rem(h + k, n_h)
-        later = jnp.minimum(t + 1, n_t - 1)
-        return remote(conv_t.at[peer], recv_t.at[1, h], cs_sem.at[1, k], cr_sem.at[1, h], (later, peer, c))
-
-    @pl.when(t < n_t - 1)
-    def _():
+    for m in range(n_t):
         for k in range(n_h):
-            to_next(k).start()
-
-    @pl.when(t == 0)
-    def _():
-        recv_t[1] = jnp.zeros_like(recv_t[1])
+            if m or k:
+                dt, peer = lax.rem(t + m, n_t), lax.rem(h + k, n_h)
+                cp = remote(conv_t.at[peer], recv_t.at[t, h], cs_sem.at[m, k], cr_sem.at[t, h], (dt, peer, c))
+                cp.start()
+                sends.append(cp)
+
+    def across_tm(f, m, j):
+        rows = pl.ds(f * columns, columns)
+        src = 2 * j + h_b
+        return remote(
+            gpad.at[1 + src, rows], gall.at[t, src, rows],
+            xs_sem.at[f * n_t + m, j], xr_sem.at[f * n_t + t, src], (lax.rem(t + m, n_t), h, c),
+        )
+
+    def to_mate(f, m, j, parity):
+        rows = pl.ds(f * columns, columns)
+        frm, src = lax.rem(t + m, n_t), 2 * j + parity
+        return remote(
+            gall.at[frm, src, rows], gall.at[frm, src, rows],
+            xs_sem.at[f * n_t + m, n_a + j], xr_sem.at[f * n_t + frm, src], (t, mate, c),
+        )
+
+    def relay(f, j):
+        for m in range(1, n_t):
+            cp = to_mate(f, m, j, h_b)
+            cp.wait_recv()
+            cp.start()
+            sends.append(cp)
 
     loads[0].wait()
     loads[1].wait()
@@ -190,61 +200,67 @@
             scaled - hidden * inverse * inverse * jnp.mean(scaled * hidden, -1, keepdims=True)
         )
         gpad[1:n_h + 1, rows, :] = g.astype(BF16).reshape(n_h, columns, chans)
+        for j in range(n_a):
+            for m in range(1, n_t):
+                cp = across_tm(f, m, j)
+                cp.start()
+                sends.append(cp)
         for item in coming[len(order):]:
             pass_on(*item)
 
-    for k in range(1, n_h):
-        src = lax.rem(h + k, n_h)
-        remote(conv_t.at[0], recv_t.at[0, src], cs_sem.at[0, k], cr_sem.at[0, src], (t, src, c)).wait_recv()
-
-    @pl.when(t > 0)
-    def _():
+    for m in range(n_t):
         for k in range(n_h):
-            src = lax.rem(h + k, n_h)
-            remote(conv_t.at[0], recv_t.at[1, src], cs_sem.at[1, k], cr_sem.at[1, src], (t, mate, c)).wait_recv()
+            if m or k:
+                frm, src = lax.rem(t + m, n_t), lax.rem(h + k, n_h)
+                remote(conv_t.at[0], recv_t.at[frm, src], cs_sem.at[m, k], cr_sem.at[frm, src], (frm, src, c)).wait_recv()
+
+    for f in range(frames - 1):
+        for j in range(n_a):
+            relay(f, j)
 
     lane = lax.broadcasted_iota(jnp.int32, (dblk, tile), 1)
-    for a in range(3):
-        for j in range(3):
-            lhs[3 * a + j, 0] = jnp.zeros((dblk, tile), BF16)
-            lhs[3 * a + j, n_h + 1] = jnp.zeros((dblk, tile), BF16)
-
-    def shifts(r, carry):
-        own = recv_t[0, r].astype(F32)
-        prev = recv_t[1, r].astype(F32)
-        both = jnp.where(lane < columns, pltpu.roll(prev, columns, 1), pltpu.roll(own, columns, 1))
-        for a, x in enumerate((prev, both, own)):
-            left = jnp.where(lax.rem(lane, columns) == 0, 0.0, pltpu.roll(x, 1, 1))
-            right = jnp.where(lax.rem(lane, columns) == columns - 1, 0.0, pltpu.roll(x, tile - 1, 1))
-            for j, y in enumerate((left, x, right)):
-                lhs[3 * a + j, r + 1] = y.astype(BF16)
-        return carry
-
-    lax.fori_loop(0, n_h, shifts, 0)
-
+    for m in range(n_t):
+        for i in range(9):
+            lhs[m, i, 0] = jnp.zeros((dblk, tile), BF16)
+            lhs[m, i, n_h + 1] = jnp.zeros((dblk, tile), BF16)
+
+    def build(m):
+        frm = lax.rem(t + m, n_t)
+        before = jnp.maximum(frm - 1, 0)
+
+        def shifts(r, carry):
+            own = recv_t[frm, r].astype(F32)
+            prev = jnp.where(frm > 0, recv_t[before, r].astype(F32), 0.0)
+            both = jnp.where(lane < columns, pltpu.roll(prev, columns, 1), pltpu.roll(own, columns, 1))
+            for a, x in enumerate((prev, both, own)):
+                left = jnp.where(lax.rem(lane, columns) == 0, 0.0, pltpu.roll(x, 1, 1))
+                right = jnp.where(lax.rem(lane, columns) == columns - 1, 0.0, pltpu.roll(x, tile - 1, 1))
+                for j, y in enumerate((left, x, right)):
+                    lhs[m, 3 * a + j, r + 1] = y.astype(BF16)
+            return carry
+
+        lax.fori_loop(0, n_h, shifts, 0)
+
+    def product(m, b, rights):
+        left = jnp.concatenate(
+            [lhs[m, :, b + r].reshape(9 * dblk, tile) for r in range(n_h)], axis=1
+        )
+        return mm(left, rights).reshape(9, dblk, chans)
+
+    build(0)
     for tap in range(27, n_b * ht):
         part_f[tap] = jnp.zeros((dblk, chans), F32)
         part_b[tap] = jnp.zeros((dblk, chans), BF16)
     rights = gpad[1:n_h + 1].reshape(n_h * tile, chans)
-    halves = [
-        remote(
-            part_b.at[pl.ds(lax.rem(c + k, n_b) * ht, ht)], got1.at[c], s1s.at[k], s1r.at[c],
-            (t, h, lax.rem(c + k, n_b)),
-        )
-        for k in range(1, n_b)
-    ]
-    sends += halves
-    for i in range(3):
-        b = jnp.where(c == 0, 2 - i, i)
-        left = jnp.concatenate(
-            [lhs[:, b + r].reshape(9 * dblk, tile) for r in range(n_h)], axis=1
-        )
-        out = (mm(left, rights) * norm).reshape(9, dblk, chans)
-        part_f[pl.ds(9 * b, 9)] = out
-        part_b[pl.ds(9 * b, 9)] = out.astype(BF16)
-        if i == (1 if n_b == 2 and ht <= 18 else 2):
-            for cp in halves:
-                cp.start()
+    spots = [(j * 3) // n_a for j in range(n_a)]
+    for b in range(3):
+        part_f[9 * b:9 * b + 9] = product(0, b, rights)
+        for j in range(n_a - 1):
+            if spots[j] == b:
+                relay(frames - 1, j)
+    for j in range(n_a - 1):
+        if spots[j] > 2:
+            relay(frames - 1, j)
 
     row = lax.broadcasted_iota(jnp.int32, (tile, chans), 0)
     for b in range(3):
@@ -262,58 +278,62 @@
         return acc
 
     y0 = taps(0)
+    relay(frames - 1, n_a - 1)
+    y1 = taps(1)
+    cut = columns
+    ig_send[...] = jnp.concatenate([y0[:cut], y0[cut:] + y1[:cut]], 0).astype(BF16)
+
+    def to_prev():
+        return remote(ig_send, ig_got, is_sem, ir_sem, (jnp.maximum(t - 1, 0), h, c))
+
+    @pl.when(t > 0)
+    def _():
+        to_prev().start()
+
+    @pl.when(t == n_t - 1)
+    def _():
+        ig_got[...] = jnp.zeros_like(ig_got)
+
+    y2 = taps(2)
+    own_ig = y2 + jnp.concatenate([y1[cut:], jnp.zeros((tile - cut, chans), F32)], 0)
+    for m in range(1, n_t):
+        build(m)
+
+    halves = [
+        remote(
+            part_b.at[pl.ds(lax.rem(c + k, n_b) * ht, ht)], got1.at[c], s1s.at[k], s1r.at[c],
+            (t, h, lax.rem(c + k, n_b)),
+        )
+        for k in range(1, n_b)
+    ]
+    sends += halves
+    for m in range(1, n_t):
+        for f in range(frames):
+            for j in range(n_a):
+                to_mate(f, m, j, 1 - h_b).wait_recv()
+    for m in range(1, max(n_t, 2)):
+        rights = gall[lax.rem(t + m, n_t)].reshape(n_h * tile, chans)
+        for i in range(3):
+            b = jnp.where(c == 0, 2 - i, i)
+            out = part_f[pl.ds(9 * b, 9)]
+            if n_t > 1:
+                out = out + product(m, b, rights)
+            if m == max(n_t, 2) - 1:
+                out = out * norm
+                part_b[pl.ds(9 * b, 9)] = out.astype(BF16)
+            part_f[pl.ds(9 * b, 9)] = out
+            if m == max(n_t, 2) - 1 and i == (1 if n_b == 2 and ht <= 18 else 2):
+                for cp in halves:
+                    cp.start()
+
     acc = part_f[pl.ds(c * ht, ht)]
     for k in range(1, n_b):
         peer = lax.rem(c + k, n_b)
         remote(part_b.at[pl.ds(0, ht)], got1.at[peer], s1s.at[k], s1r.at[peer], (t, h, peer)).wait_recv()
         acc = acc + got1[peer].astype(F32)
-    half_f[...] = acc
-    half_b[...] = acc.astype(BF16)
-    for k in range(1, n_t):
-        peer = lax.rem(t + k, n_t)
-        cp = remote(half_b.at[pl.ds(peer * tp, tp)], got2.at[t], s2s.at[k], s2r.at[t], (peer, h, c))
-        cp.start()
-        sends.append(cp)
-
-    y1 = taps(1)
-    cut = columns
-    ig_send[...] = jnp.concatenate([y0[:cut], y0[cut:] + y1[:cut]], 0).astype(BF16)
-
-    def to_prev():
-        return remote(ig_send, ig_got, is_sem, ir_sem, (jnp.maximum(t - 1, 0), h, c))
-
-    @pl.when(t > 0)
-    def _():
-        to_prev().start()
-
-    @pl.when(t == n_t - 1)
-    def _():
-        ig_got[...] = jnp.zeros_like(ig_got)
-
-    y2 = taps(2)
-    own_ig = y2 + jnp.concatenate([y1[cut:], jnp.zeros((tile - cut, chans), F32)], 0)
-
-    acc = half_f[pl.ds(t * tp, tp)]
-    for k in range(1, n_t):
-        peer = lax.rem(t + k, n_t)
-        remote(half_b.at[pl.ds(0, tp)], got2.at[peer], s2s.at[k], s2r.at[peer], (peer, h, c)).wait_recv()
-        acc = acc + got2[peer].astype(F32)
-    total[c, t] = acc.astype(BF16)
-
-    for k in range(1, n_t):
-        peer = lax.rem(t + k, n_t)
-        cp = remote(total.at[c, t], total.at[c, t], s3s.at[k], s3r.at[t], (peer, h, c))
-        cp.start()
-        sends.append(cp)
-
-    def across(piece, k):
-        return remote(
-            total.at[c, piece], total.at[c, piece], s4s.at[piece, k], s4r.at[c, piece],
-            (t, h, lax.rem(c + k, n_b)),
-        )
-
+    total[c] = acc.astype(BF16)
     for k in range(1, n_b):
-        cp = across(t, k)
+        cp = remote(total.at[c], total.at[c], s4s.at[k], s4r.at[c], (t, h, lax.rem(c + k, n_b)))
         cp.start()
         sends.append(cp)
 
@@ -323,21 +343,9 @@
 
     igrad_ref[...] = (own_ig + ig_got[...].astype(F32)).astype(BF16)
 
-    for m in range(1, n_t):
-        peer = lax.rem(t + m, n_t)
-        remote(total.at[c, peer], total.at[c, peer], s3s.at[m], s3r.at[peer], (peer, h, c)).wait_recv()
-        for k in range(1, n_b):
-            cp = across(peer, k)
-            cp.start()
-            sends.append(cp)
-    for m in range(n_t):
-        piece = lax.rem(t + m, n_t)
-        for k in range(1, n_b):
-            peer = lax.rem(c + k, n_b)
-            remote(
-                total.at[peer, piece], total.at[peer, piece], s4s.at[piece, k], s4r.at[peer, piece],
-                (t, h, peer),
-            ).wait_recv()
+    for k in range(1, n_b):
+        peer = lax.rem(c + k, n_b)
+        remote(total.at[peer], total.at[peer], s4s.at[k], s4r.at[peer], (t, h, peer)).wait_recv()
     whole = total.reshape(n_b * ht, dblk, chans)
     for a in range(3):
         for b in range(3):
@@ -345,11 +353,6 @@
 
     for cp in sends:
         cp.wait_send()
-
-    @pl.when(t < n_t - 1)
-    def _():
-        for k in range(n_h):
-            to_next(k).wait_send()
 
     @pl.when(t > 0)
     def _():
@@ -362,10 +365,9 @@
     n_t, n_h, n_b = (lax.axis_size(x) for x in ("tm", "height", "batch"))
     tile = frames * columns
     dblk = chans // n_h
-    tp = -(-27 // (n_t * n_b))
-    ht = n_t * tp
+    ht = -(-27 // n_b)
     taps = n_b * ht
-    sizes = (n_t, n_h, n_b, frames, columns, chans, tp)
+    sizes = (n_t, n_h, n_b, frames, columns, chans, ht)
     vmem = pl.BlockSpec(memory_space=pltpu.VMEM)
     hbm = pl.BlockSpec(memory_space=pl.ANY)
     dma = pltpu.SemaphoreType.DMA
@@ -383,22 +385,20 @@
             pltpu.VMEM((27, chans, chans), BF16),
             pltpu.VMEM((2, n_h, tile, chans), BF16),
             pltpu.VMEM((n_h, dblk, tile), BF16),
-            pltpu.VMEM((2, n_h, dblk, tile), BF16),
+            pltpu.VMEM((n_t, n_h, dblk, tile), BF16),
             pltpu.VMEM((n_h + 2, tile, chans), BF16),
-            pltpu.VMEM((9, n_h + 2, dblk, tile), BF16),
+            pltpu.VMEM((n_t, n_h, tile, chans), BF16),
+            pltpu.VMEM((n_t, 9, n_h + 2, dblk, tile), BF16),
             pltpu.VMEM((9, tile, chans), BF16),
             pltpu.VMEM((taps, dblk, chans), F32),
             pltpu.VMEM((taps, dblk, chans), BF16),
-            pltpu.VMEM((ht, dblk, chans), F32),
-            pltpu.VMEM((ht, dblk, chans), BF16),
             pltpu.VMEM((n_b, ht, dblk, chans), BF16),
-            pltpu.VMEM((n_t, tp, dblk, chans), BF16),
-            pltpu.VMEM((n_b, n_t, tp, dblk, chans), BF16),
+            pltpu.VMEM((n_b, ht, dblk, chans), BF16),
             pltpu.VMEM((tile, chans), BF16),
             pltpu.VMEM((tile, chans), BF16),
-            dma((3,)), dma((2 * frames, n_h)), dma((2 * frames, n_h)), dma((2, n_h)), dma((2, n_h)), dma, dma,
-            dma((n_b,)), dma((n_b,)), dma((n_t,)), dma((n_t,)), dma((n_t,)), dma((n_t,)),
-            dma((n_t, n_b)), dma((n_b, n_t)),
+            dma((3,)), dma((2 * frames, n_h)), dma((2 * frames, n_h)), dma((n_t, n_h)), dma((n_t, n_h)),
+            dma((frames * n_t, n_h)), dma((frames * n_t, n_h)), dma, dma,
+            dma((n_b,)), dma((n_b,)), dma((n_b,)), dma((n_b,)),
         ],
         compiler_params=pltpu.CompilerParams(
             collective_id=0, has_side_effects=True, vmem_limit_bytes=56 * 1024 * 1024

time: 61.8 us -> 56.8 us (0.919)
  Pallas kernels: 56.4 us -> 51.4 us
    pallas_call x1, Pallas kernels: 56.4 us -> 51.4 us  [local(): pl.pallas_call(functools.partial(body, sizes), out_shape=(jax.ShapeDtypeS...]
where the time goes in v3:
time: 56.8 us; the launch traced here: 56.6 us
  Pallas kernels  51.4 us (90%)
  other arithmetic  2.65 us (5%)
  local copies, waits for them, and re-layouts  1.89 us (3%)
  between operations  0.65 us (1%)
    pallas_call x1, Pallas kernels, local(): pl.pallas_call(functools.partial(body, sizes), out_shape=(jax.ShapeDtypeS...  51.4 us
    transpose x1, other arithmetic, local(): weight_grad = wgrad.astype(F32).transpose(1, 0, 2)  2.65 us
    reshape x1, local copies, waits for them, and re-layouts, local(): gain.reshape(1, chans)  1.25 us

profile of v3, /device:TPU:0, one launch (start us, length us, event | category | flops | bytes accessed | tf_op | source)
XLA Modules:
  0.0 56.6 jit_solution(1589931881862343441)
XLA Ops:
  0.6 1.2 %reshape.25.gain_ref = f32[1,384]{1,0:T(1,128)} reshape(f32[384]{0:T(512)} %param.10) | data formatting | bytes 3072 | tf_op jit(solution)/shard_map/reshape | solution.py:408
  1.9 51.4 %shard_map.86 = (bf16[128,384]{1,0:T(8,128)(2,1)}, bf16[27,48,384]{2,1,0:T(8,128)(2,1)}) custom-call(bf16[128,384]{1,0:T(8,128)(2,1)} %bitcast.10, bf16[128,384]{1,0:T(8,128)(2,1)} %bitcast.11, bf16[128,384]{1,0:T(8,128)(2,1)} %bitcast.12, f32[1,384]{1,0:T(1,128)} %reshape.25.gain_ref, bf16[384,1152]{1,0:T(8,128)(2,1)} %wqkv_hbm.1, ...), custom_call_target="tpu_custom_call" | custom-call | tf_op jit(solution)/shard_map/pallas_call | solution.py:374
  53.3 0.0 copy-start
  53.3 2.6 %convert_bitcast_fusion = f32[48,27,384]{2,0,1:T(8,128)} fusion(bf16[27,48,384]{2,1,0:T(8,128)(2,1)} %get-tuple-element.5), kind=kLoop, calls=%fused_computation | loop fusion | flops 497664 | bytes 2985984 | tf_op jit(solution)/shard_map/transpose | solution.py:410
  55.9 0.0 copy-done
  55.9 0.6 %copy.11 = bf16[1,2,1,64,384]{4,3,2,1,0:T(8,128)(2,1)} copy(bf16[1,2,1,64,384]{4,3,2,1,0:T(8,128)(2,1)S(1)} %bitcast.13) | data formatting | bytes 196608
Async XLA Ops:
  53.3 2.7 %copy-start = (bf16[128,384]{1,0:T(8,128)(2,1)S(1)}, bf16[128,384]{1,0:T(8,128)(2,1)}, u32[]{:S(2)}) copy-start(bf16[128,384]{1,0:T(8,128)(2,1)} %get-tuple-element.4) | copy-start | bytes 294916

commit v4 on v3

--- a/solution.py
+++ b/solution.py
@@ -92,13 +92,13 @@
 
     def send_own(f):
         for arr in range(2):
+            cp = block(f, arr, h, 0, mate, True)
+            cp.start()
+            sends.append(cp)
             for k in order:
                 cp = block(f, arr, h, k, lax.rem(h_a + k, n_a) * 2 + h_b, True)
                 cp.start()
                 sends.append(cp)
-            cp = block(f, arr, h, 0, mate, True)
-            cp.start()
-            sends.append(cp)
 
     def pass_on(f, arr, k):
         src = lax.rem(h_a + k, n_a) * 2 + h_b
@@ -294,8 +294,6 @@
     def _():
         ig_got[...] = jnp.zeros_like(ig_got)
 
-    y2 = taps(2)
-    own_ig = y2 + jnp.concatenate([y1[cut:], jnp.zeros((tile - cut, chans), F32)], 0)
     for m in range(1, n_t):
         build(m)
 
@@ -325,6 +323,9 @@
             if m == max(n_t, 2) - 1 and i == (1 if n_b == 2 and ht <= 18 else 2):
                 for cp in halves:
                     cp.start()
+
+    y2 = taps(2)
+    own_ig = y2 + jnp.concatenate([y1[cut:], jnp.zeros((tile - cut, chans), F32)], 0)
 
     acc = part_f[pl.ds(c * ht, ht)]
     for k in range(1, n_b):

time: 56.8 us -> 56.5 us (level)
  no operation moved by 1% of the time
where the time goes in v4:
time: 56.5 us; the launch traced here: 56.3 us
  Pallas kernels  51.1 us (90%)
  other arithmetic  2.65 us (5%)
  local copies, waits for them, and re-layouts  1.89 us (3%)
  between operations  0.65 us (1%)
    pallas_call x1, Pallas kernels, local(): pl.pallas_call(functools.partial(body, sizes), out_shape=(jax.ShapeDtypeS...  51.1 us
    transpose x1, other arithmetic, local(): weight_grad = wgrad.astype(F32).transpose(1, 0, 2)  2.65 us
    reshape x1, local copies, waits for them, and re-layouts, local(): gain.reshape(1, chans)  1.25 us

profile of v4, /device:TPU:0, one launch (start us, length us, event | category | flops | bytes accessed | tf_op | source)
XLA Modules:
  0.0 56.3 jit_solution(6151649576038512296)
XLA Ops:
  0.6 1.2 %reshape.25.gain_ref = f32[1,384]{1,0:T(1,128)} reshape(f32[384]{0:T(512)} %param.10) | data formatting | bytes 3072 | tf_op jit(solution)/shard_map/reshape | solution.py:409
  1.9 51.1 %shard_map.86 = (bf16[128,384]{1,0:T(8,128)(2,1)}, bf16[27,48,384]{2,1,0:T(8,128)(2,1)}) custom-call(bf16[128,384]{1,0:T(8,128)(2,1)} %bitcast.10, bf16[128,384]{1,0:T(8,128)(2,1)} %bitcast.11, bf16[128,384]{1,0:T(8,128)(2,1)} %bitcast.12, f32[1,384]{1,0:T(1,128)} %reshape.25.gain_ref, bf16[384,1152]{1,0:T(8,128)(2,1)} %wqkv_hbm.1, ...), custom_call_target="tpu_custom_call" | custom-call | tf_op jit(solution)/shard_map/pallas_call | solution.py:375
  53.0 0.0 copy-start
  53.0 2.6 %convert_bitcast_fusion = f32[48,27,384]{2,0,1:T(8,128)} fusion(bf16[27,48,384]{2,1,0:T(8,128)(2,1)} %get-tuple-element.5), kind=kLoop, calls=%fused_computation | loop fusion | flops 497664 | bytes 2985984 | tf_op jit(solution)/shard_map/transpose | solution.py:411
  55.6 0.0 copy-done
  55.6 0.6 %copy.11 = bf16[1,2,1,64,384]{4,3,2,1,0:T(8,128)(2,1)} copy(bf16[1,2,1,64,384]{4,3,2,1,0:T(8,128)(2,1)S(1)} %bitcast.13) | data formatting | bytes 196608
Async XLA Ops:
  53.0 2.7 %copy-start = (bf16[128,384]{1,0:T(8,128)(2,1)S(1)}, bf16[128,384]{1,0:T(8,128)(2,1)}, u32[]{:S(2)}) copy-start(bf16[128,384]{1,0:T(8,128)(2,1)} %get-tuple-element.4) | copy-start | bytes 294916
